TPU v7x, 32 devices: a whole 2x2x4 slice. The times are simulated.
32 devices in a mesh: region: 2 (over y), tx: 4 (over z), ty: 2 (over x), band: 2 (over core).
Axes of the slice: x: 2, y: 2, z: 4, core: 2. Of those that a mesh axis runs over, the one named last changes fastest.
Arguments:
- scenes: bfloat16 [4, 256, 12, 256], P(('region', 'ty'), 'tx', 'band'), parts along dimension 0, may hold values from -6 to 6
- cloud: bfloat16 [4, 256, 256], P(('region', 'ty'), 'tx'), parts along dimension 0, may hold values from 0.049804688 to 1
- destination: int32 [4, 256], P(('region', 'ty'), 'tx'), parts along dimension 0, may hold values from 0 to 3, as said below
- offset: int32 [4, 256], P(('region', 'ty'), 'tx'), parts along dimension 0, may hold values from 0 to 63
- counts: int32 [4, 4], P(('region', 'ty'), 'tx'), parts along dimension 0, may hold values from 32 to 64
Outputs:
- composite: bfloat16 [12, 4, 128, 512], P('band', ('region', 'ty'), 'tx'), parts along dimension 1
There are 2 independent parts, one for each index of `region`. A program takes and returns all parts, laid end to end along the dimension named above; each array names one. Nothing has to cross between parts.
Inputs may be any that keep to these rules, and one draw needn't show every extreme that they name: `destination`: among the 64 blocks of one device no tile row is named more than 32 times, and the first 32 blocks of every device in one column of tiles name one common tile row. `offset`: slots are numbered row by row, 8 slots to a row. A device's first counts blocks are live; its other blocks add nothing.
All inputs are finite; a program needn't handle non-finite values.
Results may differ from a plain program's by a relative error of at most 0.0025.
Values may be sent and summed in bfloat16 or wider, within the bound.
A program may use at most 64 MiB of HBM per device.

v0:
```python
import jax
import jax.numpy as jnp
from jax import lax
from jax.sharding import PartitionSpec as P

TS = 128
BS = 16
S_DEV = 64
MARGIN = 32
LEVELS = 4
SLOTS = 64


BINOMIAL = (0.0625, 0.25, 0.375, 0.25, 0.0625)
BACKGROUND = 0.25


def with_halo(shard, sides, width):
    for axis, dim in sides:
        devices, length = (lax.axis_size(axis), shard.shape[dim])
        up = [(i, (i + 1) % devices) for i in range(devices - 1)]
        down = [(j, i) for i, j in up]
        last = lax.slice_in_dim(shard, length - width, length, axis=dim)
        leading = lax.slice_in_dim(shard, 0, width, axis=dim)
        before = lax.ppermute(last, axis, up)
        after = lax.ppermute(leading, axis, down)
        shard = jnp.concatenate([before, shard, after], axis=dim)
    return shard


def shrink_table(length, rim_in, rim_out):
    extent = length - 2 * rim_in
    outputs = extent // 2 + 2 * rim_out
    first_index = rim_in - 2 - 2 * rim_out
    out_pos = jnp.arange(outputs, dtype=jnp.int32)[:, None]
    in_pos = jnp.arange(length, dtype=jnp.int32)[None, :]
    spacing = in_pos - first_index - 2 * out_pos
    table = jnp.zeros((outputs, length), jnp.float32)
    for tap_index, tap_weight in enumerate(BINOMIAL):
        table = table + tap_weight * (spacing == tap_index).astype(jnp.float32)
    return table


def grow_table(length, rim_in, rim_out):
    excess = 2 * rim_in - 2 - rim_out
    outputs = 2 * (length - 2) - 2 * excess
    paired = jnp.arange(outputs, dtype=jnp.int32)[:, None] + excess
    source = paired // 2
    parity = paired % 2
    spacing = jnp.arange(length, dtype=jnp.int32)[None, :] - source
    even_part = (
        0.125 * (spacing == 0).astype(jnp.float32)
        + 0.75 * (spacing == 1).astype(jnp.float32)
        + 0.125 * (spacing == 2).astype(jnp.float32)
    )
    odd_part = 0.5 * (spacing == 1).astype(jnp.float32) + 0.5 * (spacing == 2).astype(jnp.float32)
    return jnp.where(parity == 0, even_part, odd_part)


def apply_both(field, row_table, col_table):
    rows_done = jnp.einsum("ki,bic->bkc", row_table, field, precision=lax.Precision.HIGHEST)
    return jnp.einsum("bkc,mc->bkm", rows_done, col_table, precision=lax.Precision.HIGHEST)


def shrink(field, rim_in, rim_out):
    row_table = shrink_table(field.shape[-2], rim_in, rim_out)
    col_table = shrink_table(field.shape[-1], rim_in, rim_out)
    return apply_both(field, row_table, col_table)


def grow(field, rim_in, rim_out):
    row_table = grow_table(field.shape[-2], rim_in, rim_out)
    col_table = grow_table(field.shape[-1], rim_in, rim_out)
    return apply_both(field, row_table, col_table)


def trim(field, rim_have, rim_want):
    excess = rim_have - rim_want
    return field[..., excess : field.shape[-2] - excess, excess : field.shape[-1] - excess]


def border(extent, rim, begin, whole):
    position = begin - rim + jnp.arange(extent + 2 * rim, dtype=jnp.int32)
    return ((position >= 0) & (position < whole)).astype(jnp.float32)


def local(scenes, cloud, destination, offset, counts):
    row_tiles = lax.axis_size("tx")
    col_tiles = lax.axis_size("ty")
    row_tile = lax.axis_index("tx")
    col_tile = lax.axis_index("ty")
    spread = max(2, 2 * S_DEV // row_tiles)
    blocks = scenes[0]
    weights = cloud[0]
    target_row = destination[0]
    placed = offset[0]
    live_count = counts[0, 0]
    own_bands = blocks.shape[1]
    living = jnp.arange(S_DEV, dtype=jnp.int32) < live_count
    matches = (target_row[:, None] == jnp.arange(row_tiles, dtype=jnp.int32)[None, :]) & living[
        :, None
    ]
    ordinal = jnp.cumsum(matches.astype(jnp.int32), axis=0) - 1
    ranking = jnp.sum(jnp.where(matches, ordinal, 0), axis=1)
    target = target_row * spread + ranking
    chooser = (
        (jnp.arange(row_tiles * spread, dtype=jnp.int32)[:, None] == target[None, :])
        & living[None, :]
    ).astype(jnp.bfloat16)
    merged = jnp.concatenate([blocks, weights[:, None, :]], axis=1).reshape(
        S_DEV, (own_bands + 1) * BS * BS
    )
    packed = jnp.dot(chooser, merged, preferred_element_type=jnp.float32).astype(jnp.bfloat16)
    packed = packed.reshape(row_tiles, spread, own_bands + 1, BS * BS)
    slot_ids = jnp.arange(SLOTS, dtype=jnp.int32)
    tag_send = jnp.dot(
        chooser, (placed + 1).astype(jnp.bfloat16)[:, None], preferred_element_type=jnp.float32
    )
    tag_send = tag_send.astype(jnp.bfloat16).reshape(row_tiles, spread)
    arrived, tag_back = (
        lax.all_to_all(packed, "tx", split_axis=0, concat_axis=0, tiled=True),
        lax.all_to_all(tag_send, "tx", split_axis=0, concat_axis=0, tiled=True),
    )
    landing = (slot_ids + 1).astype(jnp.float32)[:, None] == tag_back.reshape(-1).astype(
        jnp.float32
    )[None, :]
    arrived = arrived.reshape(row_tiles * spread, own_bands + 1, BS * BS)
    coverage = arrived[:, own_bands:].astype(jnp.float32)
    payload = jnp.concatenate(
        [arrived[:, :own_bands].astype(jnp.float32) * coverage, coverage], axis=1
    )
    payload = payload.reshape(row_tiles * spread, (own_bands + 1) * BS * BS)
    slot_sums = jnp.dot(landing.astype(jnp.float32), payload, precision=lax.Precision.HIGHEST)
    per_row = TS // BS
    tile_field = slot_sums.reshape(per_row, per_row, own_bands + 1, BS, BS).transpose(2, 0, 3, 1, 4)
    tile_field = tile_field.reshape(own_bands + 1, TS, TS)

    def masked(field, extent, rim):
        row_mask = border(extent, rim, row_tile * extent, extent * row_tiles)
        col_mask = border(extent, rim, col_tile * extent, extent * col_tiles)
        return field * row_mask[:, None] * col_mask[None, :]

    def enlarge(field, rim_in, rim_out):
        return grow(field, rim_in, rim_out)

    ground = with_halo(tile_field, (("tx", 1), ("ty", 2)), MARGIN)
    margin = MARGIN
    needed = [0]
    for tier_index in range(1, LEVELS):
        needed.append((needed[-1] + 3) // 2)
    pyramid = [(ground, margin)]
    extent = TS
    for tier_index in range(1, LEVELS):
        source, rim_in = pyramid[-1]
        rim_out = (rim_in - 2) // 2
        extent = extent // 2
        reduced = masked(shrink(source, rim_in, rim_out), extent, rim_out)
        pyramid.append((reduced, rim_out))
    deepest = LEVELS - 1
    summit, rim_top = pyramid[-1]
    summit = trim(summit, rim_top, needed[deepest])
    collapsed = summit[:own_bands] / (BACKGROUND + summit[own_bands])
    for tier_index in range(LEVELS - 2, -1, -1):
        current, rim_here = pyramid[tier_index]
        coarser, rim_below = pyramid[tier_index + 1]
        current = trim(current, rim_here, needed[tier_index])
        detail = current[:own_bands] - enlarge(coarser[:own_bands], rim_below, needed[tier_index])
        band_part = detail / (BACKGROUND + current[own_bands])
        collapsed = band_part + enlarge(collapsed, needed[tier_index + 1], needed[tier_index])
        collapsed = masked(collapsed, TS >> tier_index, needed[tier_index])
    blended = collapsed.astype(jnp.bfloat16)
    flipped = jnp.swapaxes(blended, 1, 2)
    strips = lax.all_to_all(flipped, "tx", split_axis=1, concat_axis=2, tiled=True)
    return strips[:, None]


def solution(mesh):
    placed = (
        P(("region", "ty"), "tx", "band", None),
        P(("region", "ty"), "tx", None),
        P(("region", "ty"), "tx"),
        P(("region", "ty"), "tx"),
        P(("region", "ty"), "tx"),
    )
    return jax.shard_map(
        local,
        mesh=mesh,
        in_specs=placed,
        out_specs=P("band", ("region", "ty"), "tx", None),
        check_vma=False,
    )
```

profile of v0, /device:TPU:0, one launch (start us, length us, event | category | flops | bytes accessed | tf_op | source)
XLA Modules:
  0.0 94.9 jit_solution(7972287795352572783)
XLA Ops:
  0.7 0.7 fusion.53
  1.4 0.1 reduce_window_sum.11
  1.5 0.8 select_reduce_fusion
  2.3 0.7 fusion.167
  3.0 0.8 fusion.27
  3.8 0.7 all_to_all.26
  4.5 6.3 %all-to-all-start = ((bf16[4,1,32]{2,1,0:T(2,128)(2,1)}), bf16[4,1,32]{2,1,0:T(2,128)(2,1)S(1)}, u32[]{:S(2)}, u32[]{:S(2)}) async-start(bf16[4,1,32]{2,1,0:T(2,128)(2,1)} %all_to_all.26), calls=%async_computation | async-start | bytes 4096 | tf_op jit(solution)/shard_map/all_to_all | solution.py:122
  10.9 1.0 %maximum_bitcast_fusion = bf16[7,8,8,256]{3,2,1,0:T(8,128)(2,1)S(1)} fusion(bf16[64,1,256]{2,0,1:T(8,128)(2,1)} %bitcast.147, bf16[64,6,256]{2,0,1:T(8,128)(2,1)} %bitcast.146), kind=kLoop, calls=%fused_computation.52 | loop fusion | flops 114688 | bytes 458752
  11.9 0.3 convolution_convert_fusion
  12.2 0.5 reshape.478
  12.7 0.9 copy.71
  13.6 2.6 %all-to-all-done = bf16[4,1,32]{2,1,0:T(2,128)(2,1)S(1)} async-done(((bf16[4,1,32]{2,1,0:T(2,128)(2,1)}), bf16[4,1,32]{2,1,0:T(2,128)(2,1)S(1)}, u32[]{:S(2)}, u32[]{:S(2)}) %all-to-all-start) | async-done | bytes 288 | tf_op jit(solution)/shard_map/all_to_all | solution.py:122
  16.3 3.5 %all-to-all-start.1 = ((bf16[4,32,7,256]{3,1,2,0:T(8,128)(2,1)}), bf16[4,32,7,256]{3,1,2,0:T(8,128)(2,1)S(1)}, u32[]{:S(2)}, u32[]{:S(2)}) async-start(bf16[4,32,7,256]{3,1,2,0:T(8,128)(2,1)} %copy.71), calls=%async_computation.1 | async-start | bytes 917504 | tf_op jit(solution)/shard_map/all_to_all | solution.py:121
  19.9 0.1 reshape.482
  20.0 11.7 %all-to-all-done.1 = bf16[4,32,7,256]{3,1,2,0:T(8,128)(2,1)S(1)} async-done(((bf16[4,32,7,256]{3,1,2,0:T(8,128)(2,1)}), bf16[4,32,7,256]{3,1,2,0:T(8,128)(2,1)S(1)}, u32[]{:S(2)}, u32[]{:S(2)}) %all-to-all-start.1) | async-done | bytes 458784 | tf_op jit(solution)/shard_map/all_to_all | solution.py:121
  31.7 0.1 convert_multiply_fusion
  31.8 0.1 pad_maximum_fusion
  31.9 0.3 copy.73
  32.2 5.9 %convolution_bitcast_fusion = f32[7,8,16,8,16]{4,3,2,0,1:T(8,128)} fusion(f32[7,16,16,128,1]{3,2,1,0,4:T(8,128)S(1)} %bitcast.141, f32[128]{0:T(128)S(1)} %reshape.482, f32[8,8]{1,0:T(8,128)S(1)} %add_convert_fusion), kind=kOutput, calls=%fused_computation.1 | convolution fusion | flops 176168960 | bytes 1377024 | tf_op jit(solution)/shard_map/dot_general | solution.py:133
  38.1 4.7 %copy.99 = f32[7,8,16,8,16]{2,1,4,3,0:T(8,128)} copy(f32[7,8,16,8,16]{4,3,2,0,1:T(8,128)} %convolution_bitcast_fusion) | data formatting | bytes 917504 | tf_op jit(solution)/shard_map/reshape | solution.py:136
  42.8 2.5 %reshape.495 = f32[7,128,128]{1,2,0:T(8,128)S(1)} reshape(f32[7,8,16,8,16]{2,1,4,3,0:T(8,128)} %copy.99) | data formatting | bytes 917504 | tf_op jit(solution)/shard_map/reshape | solution.py:136
  45.3 0.0 copy-start
  45.3 1.2 %fusion.311 = (f32[7,32,128]{1,2,0:T(8,128)}, f32[7,32,128]{1,2,0:T(8,128)}) fusion(f32[7,128,128]{1,2,0:T(8,128)S(1)} %reshape.495), kind=kLoop, calls=%fused_computation.410 | loop fusion | bytes 458752 | tf_op jit(solution)/shard_map/slice | solution.py:23
  46.5 1.3 %collective-permute-start.1 = (f32[7,32,128]{1,2,0:T(8,128)}, f32[7,32,128]{1,2,0:T(8,128)}, u32[]{:S(2)}, u32[]{:S(2)}) collective-permute-start(f32[7,32,128]{1,2,0:T(8,128)} %get-tuple-element.8), channel_id=1, source_target_pairs={{4,0},{8,4},{12,8},{5,1},{9,5},{13,9},{6,2},{10,6},{14,10},{7,3},{... | collective-permute-start | bytes 344072 | tf_op jit(solution)/shard_map/ppermute | solution.py:26
  47.8 5.4 %collective-permute-start = (f32[7,32,128]{1,2,0:T(8,128)}, f32[7,32,128]{1,2,0:T(8,128)}, u32[]{:S(2)}, u32[]{:S(2)}) collective-permute-start(f32[7,32,128]{1,2,0:T(8,128)} %get-tuple-element.7), channel_id=1, source_target_pairs={{0,4},{4,8},{8,12},{1,5},{5,9},{9,13},{2,6},{6,10},{10,14},{3,7},{... | collective-permute-start | bytes 344072 | tf_op jit(solution)/shard_map/ppermute | solution.py:25
  53.2 0.0 copy-done
  53.2 0.0 slice-start
  53.2 1.9 %slice-done = f32[6,8,16,8,16]{4,3,2,0,1:T(8,128)S(1)} async-done(((f32[7,8,16,8,16]{4,3,2,0,1:T(8,128)}), f32[6,8,16,8,16]{4,3,2,0,1:T(8,128)S(1)}, s32[]{:S(2)}) %slice-start) | async-done | bytes 393240 | tf_op jit(solution)/shard_map/slice | solution.py:167
  55.1 1.9 %copy.74 = f32[6,8,16,8,16]{4,3,2,1,0:T(8,128)} copy(f32[6,8,16,8,16]{4,3,2,0,1:T(8,128)S(1)} %slice-done) | data formatting | bytes 786432 | tf_op jit(solution)/shard_map/slice | solution.py:167
  57.0 2.5 %slice.62 = f32[6,128,128]{2,1,0:T(8,128)S(1)} reshape(f32[6,8,16,8,16]{4,3,2,1,0:T(8,128)} %copy.74) | data formatting | bytes 786432 | tf_op jit(solution)/shard_map/slice | solution.py:167
  59.4 0.0 collective-permute-done.1
  59.4 0.1 collective-permute-done
  59.5 0.0 copy-done.1
  59.5 1.3 %pad_maximum_fusion.3 = (f32[7,192,32]{1,2,0:T(8,128)S(1)}, f32[7,192,32]{1,2,0:T(8,128)S(1)}) fusion(f32[7,32,128]{1,2,0:T(8,128)} %collective-permute-done.1, f32[7,128,128]{1,2,0:T(8,128)S(1)} %copy-done.1, f32[7,32,128]{1,2,0:T(8,128)} %collective-permute-done), kind=kLoop, calls=%fused_computation.51 | loop fusion | flops 172032 | bytes 1032192 | tf_op jit(solution)/shard_map/slice | solution.py:23
  60.8 1.3 %collective-permute-start.3 = (f32[7,192,32]{1,2,0:T(8,128)S(1)}, f32[7,192,32]{1,2,0:T(8,128)S(1)}, u32[]{:S(2)}, u32[]{:S(2)}) collective-permute-start(f32[7,192,32]{1,2,0:T(8,128)S(1)} %get-tuple-element.6), channel_id=1, source_target_pairs={{2,0},{3,1},{6,4},{7,5},{10,8},{11,9},{14,12},{15,13},{18,16},{19,... | collective-permute-start | bytes 516104 | tf_op jit(solution)/shard_map/ppermute | solution.py:26
  62.1 4.8 %collective-permute-start.2 = (f32[7,192,32]{1,2,0:T(8,128)S(1)}, f32[7,192,32]{1,2,0:T(8,128)S(1)}, u32[]{:S(2)}, u32[]{:S(2)}) collective-permute-start(f32[7,192,32]{1,2,0:T(8,128)S(1)} %get-tuple-element.5), channel_id=1, source_target_pairs={{0,2},{1,3},{4,6},{5,7},{8,10},{9,11},{12,14},{13,15},{16,18},{17,... | collective-permute-start | bytes 516104 | tf_op jit(solution)/shard_map/ppermute | solution.py:25
  66.9 1.1 %slice_add_fusion = f32[1,8,16,8,16]{4,3,2,0,1:T(8,128)S(1)} fusion(f32[7,8,16,8,16]{4,3,2,0,1:T(8,128)} %convolution_bitcast_fusion), kind=kLoop, calls=%fused_computation.48 | loop fusion | flops 16384 | bytes 131072 | tf_op jit(solution)/shard_map/add | solution.py:168
  68.0 0.2 add.547
  68.2 0.6 collective-permute-done.3
  68.7 1.5 %collective-permute-done.2 = f32[7,192,32]{1,2,0:T(8,128)S(1)} collective-permute-done((f32[7,192,32]{1,2,0:T(8,128)S(1)}, f32[7,192,32]{1,2,0:T(8,128)S(1)}, u32[]{:S(2)}, u32[]{:S(2)}) %collective-permute-start.2) | collective-permute-done | bytes 172064 | tf_op jit(solution)/shard_map/ppermute | solution.py:25
  70.2 2.5 %fusion.10 = f32[7,94,192]{1,2,0:T(8,128)S(1)} fusion(f32[7,192,32]{1,2,0:T(8,128)S(1)} %collective-permute-done.3, f32[7,32,128]{1,2,0:T(8,128)} %collective-permute-done.1, f32[7,128,128]{1,2,0:T(8,128)S(1)} %copy-done.1, f32[7,32,128]{1,2,0:T(8,128)} %collective-permute-done, f32[7,192,32]{1,2,0:T(8,128)S(1)} %collective-permute-done.2, ...), kind=kOutput, calls=%fused_computation.12 | convolution fusion | flops 292381056 | bytes 1537912 | tf_op jit(solution)/shard_map/ki,bic->bkc/dot_general | solution.py:61
  72.7 1.5 %fusion.16 = f32[7,94,94]{2,1,0:T(8,128)S(1)} fusion(f32[7,94,192]{1,2,0:T(8,128)S(1)} %fusion.10, f32[94]{0:T(128)S(1)} %get-tuple-element.11, f32[94]{0:T(128)S(1)} %get-tuple-element.12, s32[94]{0:T(128)S(1)} %iota_multiply_fusion.2), kind=kOutput, calls=%fused_computation.19 | convolution fusion | flops 142901440 | bytes 753880 | tf_op jit(solution)/shard_map/bkc,mc->bkm/dot_general | solution.py:62
  74.2 0.1 fusion.43
  74.3 0.4 convolution_bitcast_fusion.3
  74.7 0.4 fusion.22
  75.0 0.1 fusion.84
  75.1 0.3 convolution_bitcast_fusion.6
  75.4 0.4 fusion.26
  75.8 0.3 convolution_bitcast_fusion.7
  76.1 0.3 convolution_bitcast_fusion.8
  76.4 0.6 convolution_bitcast_fusion.1
  77.1 0.4 convolution_bitcast_fusion.4
  77.5 0.5 fusion.20
  78.0 0.4 fusion.24
  78.5 0.8 fusion.13
  79.3 0.4 fusion.25
  79.7 0.4 convolution_bitcast_fusion.5
  80.1 0.6 fusion.19
  80.6 0.5 convolution_bitcast_fusion.2
  81.2 0.8 fusion.21
  82.0 0.2 copy.86
  82.2 11.8 %all_to_all.30 = bf16[6,128,128]{2,0,1:T(8,128)(2,1)S(1)} all-to-all(bf16[6,128,128]{2,0,1:T(8,128)(2,1)S(1)} %copy.86), channel_id=1, replica_groups=mesh['region'=2,'tx'=4,'ty'=2,'band'=2] {'tx'}, dimensions={1} | all-to-all | bytes 393216 | tf_op jit(solution)/shard_map/all_to_all | solution.py:173
  94.0 0.2 copy.88
  94.2 0.8 broadcast_in_dim.136
  (28 shorter events, 0.2 us)
Async XLA Ops:
  4.5 11.8 %all-to-all-start = ((bf16[4,1,32]{2,1,0:T(2,128)(2,1)}), bf16[4,1,32]{2,1,0:T(2,128)(2,1)S(1)}, u32[]{:S(2)}, u32[]{:S(2)}) async-start(bf16[4,1,32]{2,1,0:T(2,128)(2,1)} %all_to_all.26), calls=%async_computation | async-start | bytes 4096 | tf_op jit(solution)/shard_map/all_to_all | solution.py:122
  16.3 15.4 %all-to-all-start.1 = ((bf16[4,32,7,256]{3,1,2,0:T(8,128)(2,1)}), bf16[4,32,7,256]{3,1,2,0:T(8,128)(2,1)S(1)}, u32[]{:S(2)}, u32[]{:S(2)}) async-start(bf16[4,32,7,256]{3,1,2,0:T(8,128)(2,1)} %copy.71), calls=%async_computation.1 | async-start | bytes 917504 | tf_op jit(solution)/shard_map/all_to_all | solution.py:121
  45.3 7.8 %copy-start = (f32[7,128,128]{1,2,0:T(8,128)}, f32[7,128,128]{1,2,0:T(8,128)S(1)}, u32[]{:S(2)}) copy-start(f32[7,128,128]{1,2,0:T(8,128)S(1)} %reshape.495) | copy-start | bytes 1376260
  46.5 12.9 %collective-permute-start.1 = (f32[7,32,128]{1,2,0:T(8,128)}, f32[7,32,128]{1,2,0:T(8,128)}, u32[]{:S(2)}, u32[]{:S(2)}) collective-permute-start(f32[7,32,128]{1,2,0:T(8,128)} %get-tuple-element.8), channel_id=1, source_target_pairs={{4,0},{8,4},{12,8},{5,1},{9,5},{13,9},{6,2},{10,6},{14,10},{7,3},{... | collective-permute-start | bytes 344072 | tf_op jit(solution)/shard_map/ppermute | solution.py:26
  47.8 11.7 %collective-permute-start = (f32[7,32,128]{1,2,0:T(8,128)}, f32[7,32,128]{1,2,0:T(8,128)}, u32[]{:S(2)}, u32[]{:S(2)}) collective-permute-start(f32[7,32,128]{1,2,0:T(8,128)} %get-tuple-element.7), channel_id=1, source_target_pairs={{0,4},{4,8},{8,12},{1,5},{5,9},{9,13},{2,6},{6,10},{10,14},{3,7},{... | collective-permute-start | bytes 344072 | tf_op jit(solution)/shard_map/ppermute | solution.py:25
  53.2 1.9 %slice-start = ((f32[7,8,16,8,16]{4,3,2,0,1:T(8,128)}), f32[6,8,16,8,16]{4,3,2,0,1:T(8,128)S(1)}, s32[]{:S(2)}) async-start(f32[7,8,16,8,16]{4,3,2,0,1:T(8,128)} %convolution_bitcast_fusion), calls=%async_computation.3 | async-start | bytes 6291456 | tf_op jit(solution)/shard_map/slice | solution.py:167
  57.0 2.6 %copy-start.1 = (f32[7,128,128]{1,2,0:T(8,128)S(1)}, f32[7,128,128]{1,2,0:T(8,128)}, u32[]{:S(2)}) copy-start(f32[7,128,128]{1,2,0:T(8,128)} %copy-done) | copy-start | bytes 1376260
  60.8 7.9 %collective-permute-start.3 = (f32[7,192,32]{1,2,0:T(8,128)S(1)}, f32[7,192,32]{1,2,0:T(8,128)S(1)}, u32[]{:S(2)}, u32[]{:S(2)}) collective-permute-start(f32[7,192,32]{1,2,0:T(8,128)S(1)} %get-tuple-element.6), channel_id=1, source_target_pairs={{2,0},{3,1},{6,4},{7,5},{10,8},{11,9},{14,12},{15,13},{18,16},{19,... | collective-permute-start | bytes 516104 | tf_op jit(solution)/shard_map/ppermute | solution.py:26
  62.1 8.1 %collective-permute-start.2 = (f32[7,192,32]{1,2,0:T(8,128)S(1)}, f32[7,192,32]{1,2,0:T(8,128)S(1)}, u32[]{:S(2)}, u32[]{:S(2)}) collective-permute-start(f32[7,192,32]{1,2,0:T(8,128)S(1)} %get-tuple-element.5), channel_id=1, source_target_pairs={{0,2},{1,3},{4,6},{5,7},{8,10},{9,11},{12,14},{13,15},{16,18},{17,... | collective-permute-start | bytes 516104 | tf_op jit(solution)/shard_map/ppermute | solution.py:25
where the time goes:
time: 95.5 us; the launch traced here: 94.9 us
  starting transfers between devices  22.5 us (24%)
  local copies, waits for them, and re-layouts  18.5 us (19%)
  matrix products  18.4 us (19%)
  waiting for transfers between devices  16.5 us (17%)
  blocking collectives  11.8 us (12%)
  other arithmetic  6.16 us (6%)
  between operations  1.14 us (1%)
    all_to_all x1, blocking collectives, local(): lax.all_to_all(flipped, 'tx', split_axis=1, concat_axis=2, tiled=True)  11.8 us
    all_to_all x1, waiting for transfers between devices, local(): lax.all_to_all(packed, 'tx', split_axis=0, concat_axis=0, tiled=True)  11.7 us
    ppermute x2, starting transfers between devices, with_halo(): before = lax.ppermute(last, axis, up)  10.1 us
    reshape x2, local copies, waits for them, and re-layouts, local(): tile_field = tile_field.reshape(own_bands + 1, TS, TS)  7.26 us
    all_to_all x1, starting transfers between devices, local(): lax.all_to_all(tag_send, 'tx', split_axis=0, concat_axis=0, tiled=True)  6.32 us
    slice x4, local copies, waits for them, and re-layouts, local(): current[:own_bands]  6.24 us
    dot_general x1, matrix products, local(): jnp.dot(landing.astype(jnp.float32), payload, precision=lax.Precision.HIG...  5.9 us
    dot_general x9, matrix products, apply_both(): jnp.einsum('ki,bic->bkc', row_table, field, precision=lax.Precision.HIGHEST)  5.73 us
  transfers between devices with their start and end apart: 6, of which 5 were waited for; matrix products, arithmetic and copies ran while one was open for 9% of the time, Pallas kernels for 0%

commit v1 on v0

v1 whole, which is shorter than its diff:
```python
import functools

import jax
import jax.numpy as jnp
import ml_dtypes
import numpy as np
from jax import lax
from jax.experimental import pallas as pl
from jax.experimental.pallas import tpu as pltpu
from jax.sharding import PartitionSpec as P

TS = 128
BS = 16
S_DEV = 64
SLOTS = 64
TAPS = (0.0625, 0.25, 0.375, 0.25, 0.0625)
BACKGROUND = 0.25
MESH = pl.DeviceIdType.MESH
BF = jnp.bfloat16
F32 = jnp.float32
REACH = {1: (-1, 64), 2: (-1, 33), 3: (-1, 17)}


def stack_order():
    left, right, rest = [], [], []
    for level, (first, last) in REACH.items():
        width = 2 * (2**level - 1)
        for p in range(first, last + 1):
            entry = (level, p)
            if 2**level * p - width < 0:
                left.append(entry)
            elif 2**level * p + width >= TS:
                right.append(entry)
            else:
                rest.append(entry)
    assert len(left) == 8 and len(right) == 8 and len(rest) <= 112
    return left + right + rest


def operators(is_first, is_last):
    order = stack_order()
    low, high = (0 if is_first else -TS), (TS if is_last else 2 * TS)
    down = {0: np.eye(3 * TS)}
    begin = {0: -TS}
    for p in range(3 * TS):
        if not low <= p - TS < high:
            down[0][p] = 0
    for level in (1, 2, 3):
        extent = 3 * TS >> level
        begin[level] = -(TS >> level)
        matrix = np.zeros((extent, 3 * TS))
        for i in range(extent):
            p = begin[level] + i
            if not (low >> level) <= p < (high >> level):
                continue
            for a, tap in enumerate(TAPS):
                source = 2 * p + a - 2 - begin[level - 1]
                if 0 <= source < down[level - 1].shape[0]:
                    matrix[i] += tap * down[level - 1][source]
        down[level] = matrix
    where = {entry: i for i, entry in enumerate(order)}
    d = np.zeros((TS, 3 * TS))
    for (level, p), i in where.items():
        d[i] = down[level][p - begin[level]]

    def grown(p):
        half = p // 2
        if p % 2 == 0:
            return ((half - 1, 0.125), (half, 0.75), (half + 1, 0.125))
        return ((half, 0.5), (half + 1, 0.5))

    up = np.zeros((TS, TS))
    for (level, p), i in where.items():
        if level < 3 and (low >> level) <= p < (high >> level):
            for q, weight in grown(p):
                up[i, where[(level + 1, q)]] += weight
    f = np.zeros((TS, TS))
    for p in range(TS):
        for q, weight in grown(p):
            f[p, where[(1, q)]] += weight
    q = f @ (np.eye(TS) + up + up @ up)
    return d, up, f, q


def bf16(x):
    return x.astype(ml_dtypes.bfloat16)


def tables():
    order = stack_order()
    levels = np.array([level for level, _ in order] + [0] * (TS - len(order)))
    same = ((levels[:, None] == levels[None, :]) & (levels[:, None] > 0)).astype(np.float32)
    dc, pc, qc, dr, pfr, qr = [], [], [], [], [], []
    for variant in range(4):
        d, up, f, q = operators(variant % 2 == 1, variant >= 2)
        mid = operators(False, False)[0]
        to_left = mid[8:16, 2 * TS :]
        to_right = mid[0:8, :TS]
        edges = np.concatenate([to_left, to_right])
        own = np.concatenate([d[:, TS : 2 * TS], edges])
        top = bf16(own).astype(np.float64)
        low = own - top
        three = np.concatenate([top, top, low], axis=1)
        assert np.all(bf16(low).astype(np.float64) == low)
        assert np.all(bf16(up).astype(np.float64) == up)
        q_top = bf16(q).astype(np.float64)
        q_three = np.concatenate([q_top, q_top, q - q_top], axis=1)
        dc.append(three)
        dr.append(three[:TS].T)
        pc.append(np.concatenate([up, up], axis=1))
        qc.append(q_three)
        pf = np.concatenate([up.T, f.T], axis=1)
        pfr.append(np.concatenate([pf, pf], axis=0))
        qr.append(q_three.T)
    de = dc[0][TS:]
    fc = np.concatenate([f, f], axis=1)
    return [bf16(np.stack(x)) for x in (dc, pc, qc, dr, pfr, qr)] + [bf16(de), bf16(fc), same]


def split(x, axis, three=False):
    top = x.astype(BF)
    low = (x - top.astype(F32)).astype(BF)
    return jnp.concatenate([top, low, top] if three else [top, low], axis=axis)


def dot(a, b):
    return jnp.dot(a, b, preferred_element_type=F32)


def regroup(x):
    row = lax.broadcasted_iota(jnp.int32, x.shape, 1)
    col = lax.broadcasted_iota(jnp.int32, x.shape, 2) // BS
    for d in (4, 2, 1):
        row_bit, col_bit = (row // d) % 2, (col // d) % 2
        ahead = pltpu.roll(pltpu.roll(x, 8 - d, 1), BS * d, 2)
        if d == 4:
            x = jnp.where(row_bit == col_bit, x, ahead)
        else:
            behind = pltpu.roll(pltpu.roll(x, d, 1), TS - BS * d, 2)
            x = jnp.where(row_bit == col_bit, x, jnp.where(row_bit == 0, ahead, behind))
    return x


def kernel(
    n_tx, n_ty, own, spread, rows, strip, strip_rows,
    scenes, cloud, destination, offset, counts, same,
    dc_h, pc_h, qc_h, dr_h, pfr_h, qr_h, de_h, fc_h,
    out,
    dc, pc, qc, dr, pfr, qr, de, fc,
    merged, sent, landed, code_out, code_in, field, cols_out, cols_in, rows_out, rows_in,
    final, staged, strip_out, strip_in,
    const_sem, block_send, block_recv, code_send, code_recv, halo_send, halo_recv, strip_send, strip_recv,
):
    me, col = lax.axis_index("tx"), lax.axis_index("ty")
    chans = own + 1
    variant_c = jnp.where(col == 0, 1, 0) + jnp.where(col == n_ty - 1, 2, 0)
    variant_r = jnp.where(me == 0, 1, 0) + jnp.where(me == n_tx - 1, 2, 0)

    barrier = pltpu.get_barrier_semaphore()
    for d in range(1, n_tx):
        pl.semaphore_signal(barrier, inc=1, device_id={"tx": lax.rem(me + d, n_tx)}, device_id_type=MESH)

    @pl.when(col > 0)
    def _():
        pl.semaphore_signal(barrier, inc=1, device_id={"ty": col - 1}, device_id_type=MESH)

    @pl.when(col < n_ty - 1)
    def _():
        pl.semaphore_signal(barrier, inc=1, device_id={"ty": col + 1}, device_id_type=MESH)

    loads = [
        pltpu.make_async_copy(src, dst, const_sem.at[i])
        for i, (src, dst) in enumerate(
            (
                (dc_h.at[variant_c], dc), (pc_h.at[variant_c], pc), (qc_h.at[variant_c], qc),
                (dr_h.at[variant_r], dr), (pfr_h.at[variant_r], pfr), (qr_h.at[variant_r], qr),
                (de_h, de), (fc_h, fc),
            )
        )
    ]
    for load in loads:
        load.start()

    dest = jnp.broadcast_to(destination[...], (S_DEV, S_DEV))
    dest_t = dest.T
    lane = lax.broadcasted_iota(jnp.int32, (S_DEV, S_DEV), 1)
    sub = lax.broadcasted_iota(jnp.int32, (S_DEV, S_DEV), 0)
    live = jnp.broadcast_to(counts[...], (S_DEV, S_DEV))
    earlier = (dest == dest_t) & (sub < lane)
    rank = jnp.sum(jnp.where(earlier, 1.0, 0.0), axis=0, keepdims=True)
    target = jnp.where(lane[:1] < live[:1], dest[:1].astype(F32) * spread + rank, -1.0)
    wide = lax.broadcasted_iota(jnp.int32, (S_DEV, 8 * S_DEV), 1)
    spread_out = jnp.where(wide // 8 == lax.broadcasted_iota(jnp.int32, wide.shape, 0), 1.0, 0.0).astype(BF)
    key = dot(jnp.broadcast_to(target, (16, S_DEV)).astype(BF), spread_out)[:1]
    key = jnp.where(key < 0, -1.0, key + 256.0 * (wide[:1] % 8).astype(F32))

    merged[...] = jnp.zeros_like(merged)
    for half in range(2):
        at = slice(half * TS, half * TS + TS)
        for b in range(own):
            merged[half, pl.ds(b, S_DEV, stride=8), :] = scenes[0, :, b, at].astype(F32)
        merged[half, pl.ds(own, S_DEV, stride=8), :] = cloud[0, :, at].astype(F32)
    everything = jnp.concatenate([merged[0], merged[1]], axis=1).astype(BF)
    line = lax.broadcasted_iota(jnp.int32, (rows, 1), 0)

    code_lanes = code_out.shape[2]
    lanes = lax.broadcasted_iota(jnp.int32, (S_DEV, code_lanes), 1)
    rank_t = jnp.broadcast_to(rank, (S_DEV, S_DEV)).T[:, :1]
    seat = jnp.where((lanes % spread).astype(F32) == rank_t, 1.0, 0.0).astype(BF)
    tall = lax.broadcasted_iota(jnp.int32, (max(16, n_tx), S_DEV), 0)
    across = lax.broadcasted_iota(jnp.int32, tall.shape, 1)
    marks = jnp.where((tall == destination[...]) & (across < counts[...]), (offset[...] + 1).astype(F32), 0.0)
    codes = dot(marks.astype(BF), seat) + 128.0 * (lanes[:1] // spread).astype(F32)
    for t in range(n_tx):
        code_out[t] = jnp.broadcast_to(codes[t : t + 1], (8, code_lanes))

    def pack(t):
        slot = t * spread + line % spread
        line_key = (256 * (line // spread) + slot).astype(F32)
        chooser = jnp.where(line_key == key, 1.0, 0.0).astype(BF)
        return dot(chooser, everything).astype(BF)

    pl.semaphore_wait(barrier, n_tx - 1 + jnp.where(col > 0, 1, 0) + jnp.where(col < n_ty - 1, 1, 0))

    def exchange(src, dst, send, recv, other):
        return pltpu.make_async_remote_copy(
            src_ref=src.at[other], dst_ref=dst.at[me], send_sem=send.at[other], recv_sem=recv.at[me],
            device_id={"tx": other}, device_id_type=MESH,
        )

    def incoming(src, dst, send, recv, other):
        return pltpu.make_async_remote_copy(
            src_ref=src.at[other], dst_ref=dst.at[other], send_sem=send.at[other], recv_sem=recv.at[other],
            device_id={"tx": other}, device_id_type=MESH,
        )

    peers = [lax.rem(me + d, n_tx) for d in range(1, n_tx)]
    for peer in peers:
        exchange(code_out, code_in, code_send, code_recv, peer).start()
        sent[peer] = pack(peer)
        exchange(sent, landed, block_send, block_recv, peer).start()

    row_code = lax.broadcasted_iota(jnp.int32, (chans * SLOTS, 1), 0)
    row_code = (128 * (row_code // SLOTS) + row_code % SLOTS + 1).astype(F32)
    here = lax.broadcasted_iota(jnp.int32, (rows, rows), 0)
    there = lax.broadcasted_iota(jnp.int32, (rows, rows), 1)
    cover_of = jnp.where(there == own * spread + here % spread, 1.0, 0.0).astype(BF)

    def place(block, code):
        values = block.astype(F32)
        if spread % 8 == 0:
            cover = values[own * spread :]
            product = jnp.concatenate([values[: own * spread] * jnp.concatenate([cover] * own), cover])
        else:
            cover = dot(cover_of, block)
            product = values * jnp.where(line >= own * spread, 1.0, cover)
        landing = jnp.where(row_code == code, 1.0, 0.0).astype(BF)
        top = product.astype(BF)
        low = (product - top.astype(F32)).astype(BF)
        return dot(landing, top) + dot(landing, low)

    total = place(pack(me), code_out[me][:1, :rows])
    for peer in peers:
        incoming(code_out, code_in, code_send, code_recv, peer).wait_recv()
        incoming(sent, landed, block_send, block_recv, peer).wait_recv()
        total += place(landed[peer], code_in[peer][:1, :rows])

    per_row = TS // BS
    for half in range(2):
        part = total[:, half * TS : half * TS + TS].reshape(chans * per_row, 8, TS)
        field[:, :, half] = regroup(part).reshape(chans, per_row, 8, TS)

    for load in loads:
        load.wait()

    tiles = []
    stack = []
    for c in range(chans):
        tile = field[c].reshape(TS, TS).T
        tiles.append(tile)
        got = dot(dc[...], split(tile, 0, three=True))
        stack.append(got[:TS])
        cols_out[0, c] = got[TS : TS + 8]
        cols_out[1, c] = got[TS + 8 : TS + 16]

    def halo(axis, src, dst, side, place_at, other):
        return pltpu.make_async_remote_copy(
            src_ref=src.at[side], dst_ref=dst.at[1 - side], send_sem=halo_send.at[place_at + side],
            recv_sem=halo_recv.at[place_at + 1 - side], device_id={axis: other}, device_id_type=MESH,
        )

    def swap(axis, at, n, src, dst, place_at):
        @pl.when(at > 0)
        def _():
            halo(axis, src, dst, 0, place_at, at - 1).start()

        @pl.when(at < n - 1)
        def _():
            halo(axis, src, dst, 1, place_at, at + 1).start()

        @pl.when(at == 0)
        def _():
            dst[0] = jnp.zeros_like(dst[0])

        @pl.when(at == n - 1)
        def _():
            dst[1] = jnp.zeros_like(dst[1])

    def swapped(axis, at, n, src, dst, place_at):
        @pl.when(at > 0)
        def _():
            halo(axis, src, dst, 0, place_at, at - 1).wait_send()
            halo(axis, src, dst, 1, place_at, at - 1).wait_recv()

        @pl.when(at < n - 1)
        def _():
            halo(axis, src, dst, 1, place_at, at + 1).wait_send()
            halo(axis, src, dst, 0, place_at, at + 1).wait_recv()

    swap("ty", col, n_ty, cols_out, cols_in, 0)
    swapped("ty", col, n_ty, cols_out, cols_in, 0)
    for c in range(chans):
        stack[c] = jnp.concatenate([stack[c][:8] + cols_in[0, c], stack[c][8:16] + cols_in[1, c], stack[c][16:]], axis=0)

    flat = split(jnp.concatenate(stack, axis=0), 1, three=True)
    edges = lax.dot_general(de[...], flat, (((1,), (1,)), ((), ())), preferred_element_type=F32)
    rows_out[0] = edges[:8]
    rows_out[1] = edges[8:]
    swap("tx", me, n_tx, rows_out, rows_in, 2)
    deep = dot(flat, dr[...])
    swapped("tx", me, n_tx, rows_out, rows_in, 2)
    rim = jnp.concatenate([rows_in[0], rows_in[1], jnp.zeros((TS - 16, chans * TS), F32)], axis=0)
    deep = deep + rim.T

    weight = deep[own * TS :]
    detail = split(dot(split(deep[: own * TS], 1), pfr[...]), 1)
    scale = same[...] / (BACKGROUND + weight)
    bands = []
    finer = []
    for b in range(own):
        at = slice(b * TS, b * TS + TS)
        both = jnp.concatenate([detail[at, : 2 * TS], detail[at, 2 * TS :]], axis=0)
        bands.append((deep[at] - dot(pc[...], both[:, :TS])) * scale)
        finer.append(dot(fc[...], both[:, TS:]))
    lifted = dot(split(jnp.concatenate(bands, axis=0), 1, three=True), qr[...])
    share = 1.0 / (BACKGROUND + tiles[own])
    for b in range(own):
        at = slice(b * TS, b * TS + TS)
        final[b] = (tiles[b] - finer[b]) * share + dot(qc[...], split(lifted[at], 0, three=True))

    def strip_of(t):
        for b in range(own):
            staged[b * strip : (b + 1) * strip, :] = final[b, pl.ds(t * strip, strip), :]
        return staged[...].astype(BF)

    staged[...] = jnp.zeros_like(staged)
    for peer in peers:
        strip_out[peer] = strip_of(peer)
        exchange(strip_out, strip_in, strip_send, strip_recv, peer).start()
    strip_in[me] = strip_of(me)
    for peer in peers:
        incoming(strip_out, strip_in, strip_send, strip_recv, peer).wait_recv()
    for s in range(n_tx):
        got = strip_in[s].astype(F32)
        for b in range(own):
            out[b, 0, :, s * TS : (s + 1) * TS] = got[b * strip : (b + 1) * strip].astype(BF)
    for peer in peers:
        exchange(code_out, code_in, code_send, code_recv, peer).wait_send()
        exchange(sent, landed, block_send, block_recv, peer).wait_send()
        exchange(strip_out, strip_in, strip_send, strip_recv, peer).wait_send()


def solution(mesh):
    n_tx, n_ty = mesh.shape["tx"], mesh.shape["ty"]
    consts = tables()

    def local(scenes, cloud, destination, offset, counts):
        own = scenes.shape[2]
        chans = own + 1
        spread = max(2, 2 * S_DEV // n_tx)
        rows = -(-chans * spread // 16) * 16
        code_lanes = -(-rows // TS) * TS
        strip = TS // n_tx
        strip_rows = -(-own * strip // 16) * 16
        moved = consts[:6]
        fixed = consts[6:8]
        vmem = pl.BlockSpec(memory_space=pltpu.VMEM)
        return pl.pallas_call(
            functools.partial(kernel, n_tx, n_ty, own, spread, rows, strip, strip_rows),
            out_shape=jax.ShapeDtypeStruct((own, 1, strip, TS * n_tx), BF),
            in_specs=[vmem] * 6 + [pl.BlockSpec(memory_space=pl.ANY)] * 8,
            out_specs=vmem,
            scratch_shapes=[pltpu.VMEM(x.shape[1:], BF) for x in moved]
            + [pltpu.VMEM(x.shape, BF) for x in fixed]
            + [
                pltpu.VMEM((2, 8 * S_DEV, TS), F32),
                pltpu.VMEM((n_tx, rows, BS * BS), BF),
                pltpu.VMEM((n_tx, rows, BS * BS), BF),
                pltpu.VMEM((n_tx, 8, code_lanes), F32),
                pltpu.VMEM((n_tx, 8, code_lanes), F32),
                pltpu.VMEM((chans, TS // BS, 2, 8, TS), F32),
                pltpu.VMEM((2, chans, 8, TS), F32),
                pltpu.VMEM((2, chans, 8, TS), F32),
                pltpu.VMEM((2, 8, chans * TS), F32),
                pltpu.VMEM((2, 8, chans * TS), F32),
                pltpu.VMEM((own, TS, TS), F32),
                pltpu.VMEM((strip_rows, TS), F32),
                pltpu.VMEM((n_tx, strip_rows, TS), BF),
                pltpu.VMEM((n_tx, strip_rows, TS), BF),
                pltpu.SemaphoreType.DMA((8,)),
            ]
            + [pltpu.SemaphoreType.DMA((n_tx,))] * 4
            + [pltpu.SemaphoreType.DMA((4,))] * 2
            + [pltpu.SemaphoreType.DMA((n_tx,))] * 2,
            compiler_params=pltpu.CompilerParams(
                collective_id=0, has_side_effects=True, vmem_limit_bytes=48 * 1024 * 1024
            ),
        )(scenes, cloud, destination, offset, counts, jnp.asarray(consts[8]), *(jnp.asarray(x) for x in moved + fixed))

    placed = (
        P(("region", "ty"), "tx", "band", None),
        P(("region", "ty"), "tx", None),
        P(("region", "ty"), "tx"),
        P(("region", "ty"), "tx"),
        P(("region", "ty"), "tx"),
    )
    return jax.shard_map(
        local, mesh=mesh, in_specs=placed, out_specs=P("band", ("region", "ty"), "tx", None), check_vma=False
    )
```

time: 95.5 us -> 41.6 us (0.44)
  Pallas kernels: 0 us -> 31.2 us
  starting transfers between devices: 22.5 us -> 0 us
  matrix products: 18.4 us -> 0 us
  waiting for transfers between devices: 16.5 us -> 0 us
  blocking collectives: 11.8 us -> 0 us
  local copies, waits for them, and re-layouts: 18.5 us -> 9.17 us
  other arithmetic: 6.16 us -> 0 us
    pallas_call x0 -> x1, Pallas kernels: none -> 31.2 us  [local(): pl.pallas_call(functools.partial(kernel, n_tx, n_ty, own, spread, rows, s...]
    dot_general x21 -> x0, matrix products: 18.4 us -> none  [the longest x1 5.9 us: local(): jnp.dot(landing.astype(jnp.float32), payload, precision=lax.Precision.HIG...]
    all_to_all x2 -> x0, waiting for transfers between devices: 14.3 us -> none  [the longest x1 11.7 us: local(): lax.all_to_all(packed, 'tx', split_axis=0, concat_axis=0, tiled=True)]
    ppermute x4 -> x0, starting transfers between devices: 12.7 us -> none  [the longest x2 10.1 us: with_halo(): before = lax.ppermute(last, axis, up)]
    all_to_all x1 -> x0, blocking collectives: 11.8 us -> none  [local(): lax.all_to_all(flipped, 'tx', split_axis=1, concat_axis=2, tiled=True)]
    all_to_all x2 -> x0, starting transfers between devices: 9.78 us -> none  [the longest x1 6.32 us: local(): lax.all_to_all(tag_send, 'tx', split_axis=0, concat_axis=0, tiled=True)]
    unnamed x4 -> x26, local copies, waits for them, and re-layouts: 0.01 us -> 9.17 us
    reshape x5 -> x0, local copies, waits for them, and re-layouts: 8.68 us -> none  [the longest x2 7.26 us: local(): tile_field = tile_field.reshape(own_bands + 1, TS, TS)]
  transfers between devices with their start and end apart: 6 -> 0, of which waited for: 5 -> 0; matrix products, arithmetic and copies ran while one was open for 9% -> 0% of each run, Pallas kernels for 0% -> 0%
where the time goes in v1:
time: 41.6 us; the launch traced here: 41.1 us
  Pallas kernels  31.2 us (75%)
  local copies, waits for them, and re-layouts  9.17 us (22%)
  between operations  0.79 us (2%)
    pallas_call x1, Pallas kernels, local(): pl.pallas_call(functools.partial(kernel, n_tx, n_ty, own, spread, rows, s...  31.2 us
    unnamed x26, local copies, waits for them, and re-layouts  9.17 us

profile of v1, /device:TPU:0, one launch (start us, length us, event | category | flops | bytes accessed | tf_op | source)
XLA Modules:
  0.0 41.1 jit_solution(1410496676278363085)
XLA Ops:
  0.0 0.0 copy-start.1
  0.7 0.0 copy-start.9
  0.7 0.0 copy-start.10
  0.7 0.0 copy-start.11
  0.7 1.1 %copy.15.scenes = bf16[1,64,6,256]{3,2,1,0:T(8,128)(2,1)S(1)} copy(bf16[1,64,6,256]{3,1,2,0:T(8,128)(2,1)} %param.14) | data formatting | bytes 393216 | tf_op args[0]
  1.8 0.0 copy-done.1
  1.8 0.0 copy-done.9
  1.8 0.0 copy-done.10
  1.8 0.0 copy-done.11
  1.8 0.0 copy-start
  1.9 1.0 %copy-done = bf16[4,256,256]{2,1,0:T(8,128)(2,1)S(1)} copy-done((bf16[4,256,256]{2,1,0:T(8,128)(2,1)S(1)}, bf16[4,256,256]{2,1,0:T(8,128)(2,1)}, u32[]{:S(2)}) %copy-start) | copy-done | bytes 524312
  2.9 0.0 copy-start.2
  2.9 1.0 %copy-done.2 = bf16[4,384,128]{2,1,0:T(8,128)(2,1)S(1)} copy-done((bf16[4,384,128]{2,1,0:T(8,128)(2,1)S(1)}, bf16[4,384,128]{2,1,0:T(8,128)(2,1)}, u32[]{:S(2)}) %copy-start.2) | copy-done | bytes 393240
  3.9 0.0 copy-start.3
  3.9 1.0 %copy-done.3 = bf16[4,384,128]{2,1,0:T(8,128)(2,1)S(1)} copy-done((bf16[4,384,128]{2,1,0:T(8,128)(2,1)S(1)}, bf16[4,384,128]{2,1,0:T(8,128)(2,1)}, u32[]{:S(2)}) %copy-start.3) | copy-done | bytes 393240
  4.9 0.0 copy-start.4
  4.9 1.0 %copy-done.4 = bf16[4,128,384]{2,1,0:T(8,128)(2,1)S(1)} copy-done((bf16[4,128,384]{2,1,0:T(8,128)(2,1)S(1)}, bf16[4,128,384]{2,1,0:T(8,128)(2,1)}, u32[]{:S(2)}) %copy-start.4) | copy-done | bytes 393240
  5.9 0.0 copy-start.5
  5.9 0.9 %copy-done.5 = bf16[4,128,256]{2,1,0:T(8,128)(2,1)S(1)} copy-done((bf16[4,128,256]{2,1,0:T(8,128)(2,1)S(1)}, bf16[4,128,256]{2,1,0:T(8,128)(2,1)}, u32[]{:S(2)}) %copy-start.5) | copy-done | bytes 262168
  6.8 0.0 copy-start.6
  6.8 0.8 %copy-done.6 = bf16[128,256]{1,0:T(8,128)(2,1)S(1)} copy-done((bf16[128,256]{1,0:T(8,128)(2,1)S(1)}, bf16[128,256]{1,0:T(8,128)(2,1)}, u32[]{:S(2)}) %copy-start.6) | copy-done | bytes 65560
  7.7 0.0 copy-start.7
  7.7 0.8 %copy-done.7 = f32[128,128]{1,0:T(8,128)S(1)} copy-done((f32[128,128]{1,0:T(8,128)S(1)}, f32[128,128]{1,0:T(8,128)}, u32[]{:S(2)}) %copy-start.7) | copy-done | bytes 65560
  8.5 0.0 copy-start.8
  8.5 0.8 %copy-done.8 = bf16[1,64,256]{2,1,0:T(8,128)(2,1)S(1)} copy-done((bf16[1,64,256]{2,1,0:T(8,128)(2,1)S(1)}, bf16[1,64,256]{2,1,0:T(8,128)(2,1)}, u32[]{:S(2)}) %copy-start.8) | copy-done | bytes 32792
  9.3 31.2 %shard_map.136 = bf16[6,1,32,512]{3,2,1,0:T(8,128)(2,1)S(1)} custom-call(bf16[1,64,6,256]{3,2,1,0:T(8,128)(2,1)S(1)} %copy.15.scenes, bf16[1,64,256]{2,1,0:T(8,128)(2,1)S(1)} %copy-done.8, s32[1,64]{1,0:T(1,128)S(1)} %copy-done.10, s32[1,64]{1,0:T(1,128)S(1)} %copy-done.11, s32[1,1]{1,0:T(1,128)S(6)} %copy.17.counts, f32[128,128]{1,0:T(8,128)S(1)} %copy-done.7, ...), custom_call_target="tpu_custom_call" | custom-call | tf_op jit(solution)/shard_map/pallas_call | solution.py:388
  40.4 0.7 %copy.18 = bf16[6,1,32,512]{3,2,1,0:T(8,128)(2,1)} copy(bf16[6,1,32,512]{3,2,1,0:T(8,128)(2,1)S(1)} %shard_map.136) | data formatting | bytes 393216
Async XLA Ops:
  0.0 1.8 %copy-start.1 = (bf16[4,144,384]{2,1,0:T(8,128)(2,1)S(1)}, bf16[4,144,384]{2,1,0:T(8,128)(2,1)}, u32[]{:S(2)}) copy-start(bf16[4,144,384]{2,1,0:T(8,128)(2,1)} %constant.19.clone.dc_h) | copy-start | bytes 1327108
  0.7 1.1 %copy-start.9 = (bf16[16,384]{1,0:T(8,128)(2,1)S(1)}, bf16[16,384]{1,0:T(8,128)(2,1)}, u32[]{:S(2)}) copy-start(bf16[16,384]{1,0:T(8,128)(2,1)} %constant.25.clone.de_h) | copy-start | bytes 36868
  0.7 1.1 %copy-start.10 = (s32[1,64]{1,0:T(1,128)S(1)}, s32[1,64]{1,0:T(1,128)}, u32[]{:S(2)}) copy-start(s32[1,64]{1,0:T(1,128)} %destination.1) | copy-start | bytes 772
  0.7 1.1 %copy-start.11 = (s32[1,64]{1,0:T(1,128)S(1)}, s32[1,64]{1,0:T(1,128)}, u32[]{:S(2)}) copy-start(s32[1,64]{1,0:T(1,128)} %offset.1) | copy-start | bytes 772
  1.8 1.0 %copy-start = (bf16[4,256,256]{2,1,0:T(8,128)(2,1)S(1)}, bf16[4,256,256]{2,1,0:T(8,128)(2,1)}, u32[]{:S(2)}) copy-start(bf16[4,256,256]{2,1,0:T(8,128)(2,1)} %constant.23.clone.pfr_h) | copy-start | bytes 1572868
  2.9 1.0 %copy-start.2 = (bf16[4,384,128]{2,1,0:T(8,128)(2,1)S(1)}, bf16[4,384,128]{2,1,0:T(8,128)(2,1)}, u32[]{:S(2)}) copy-start(bf16[4,384,128]{2,1,0:T(8,128)(2,1)} %constant.24.clone.qr_h) | copy-start | bytes 1179652
  3.9 1.0 %copy-start.3 = (bf16[4,384,128]{2,1,0:T(8,128)(2,1)S(1)}, bf16[4,384,128]{2,1,0:T(8,128)(2,1)}, u32[]{:S(2)}) copy-start(bf16[4,384,128]{2,1,0:T(8,128)(2,1)} %constant.22.clone.dr_h) | copy-start | bytes 1179652
  4.9 1.0 %copy-start.4 = (bf16[4,128,384]{2,1,0:T(8,128)(2,1)S(1)}, bf16[4,128,384]{2,1,0:T(8,128)(2,1)}, u32[]{:S(2)}) copy-start(bf16[4,128,384]{2,1,0:T(8,128)(2,1)} %constant.21.clone.qc_h) | copy-start | bytes 1179652
  5.9 0.9 %copy-start.5 = (bf16[4,128,256]{2,1,0:T(8,128)(2,1)S(1)}, bf16[4,128,256]{2,1,0:T(8,128)(2,1)}, u32[]{:S(2)}) copy-start(bf16[4,128,256]{2,1,0:T(8,128)(2,1)} %constant.20.clone.pc_h) | copy-start | bytes 786436
  6.8 0.8 %copy-start.6 = (bf16[128,256]{1,0:T(8,128)(2,1)S(1)}, bf16[128,256]{1,0:T(8,128)(2,1)}, u32[]{:S(2)}) copy-start(bf16[128,256]{1,0:T(8,128)(2,1)} %constant.26.clone.fc_h) | copy-start | bytes 196612
  7.7 0.8 %copy-start.7 = (f32[128,128]{1,0:T(8,128)S(1)}, f32[128,128]{1,0:T(8,128)}, u32[]{:S(2)}) copy-start(f32[128,128]{1,0:T(8,128)} %constant.18.clone.same) | copy-start | bytes 196612
  8.5 0.8 %copy-start.8 = (bf16[1,64,256]{2,1,0:T(8,128)(2,1)S(1)}, bf16[1,64,256]{2,1,0:T(8,128)(2,1)}, u32[]{:S(2)}) copy-start(bf16[1,64,256]{2,1,0:T(8,128)(2,1)} %cloud.1) | copy-start | bytes 98308

commit v2 on v1

v2 whole, which is shorter than its diff:
```python
import functools

import jax
import jax.numpy as jnp
import ml_dtypes
import numpy as np
from jax import lax
from jax.experimental import pallas as pl
from jax.experimental.pallas import tpu as pltpu
from jax.sharding import PartitionSpec as P

TS = 128
BS = 16
S_DEV = 64
SLOTS = 64
TAPS = (0.0625, 0.25, 0.375, 0.25, 0.0625)
BACKGROUND = 0.25
MESH = pl.DeviceIdType.MESH
BF = jnp.bfloat16
F32 = jnp.float32
REACH = {1: (-1, 64), 2: (-1, 33), 3: (-1, 17)}


def stack_order():
    left, right, rest = [], [], []
    for level, (first, last) in REACH.items():
        width = 2 * (2**level - 1)
        for p in range(first, last + 1):
            entry = (level, p)
            if 2**level * p - width < 0:
                left.append(entry)
            elif 2**level * p + width >= TS:
                right.append(entry)
            else:
                rest.append(entry)
    assert len(left) == 8 and len(right) == 8 and len(rest) <= 112
    return left + right + rest


def operators(is_first, is_last):
    order = stack_order()
    low, high = (0 if is_first else -TS), (TS if is_last else 2 * TS)
    down = {0: np.eye(3 * TS)}
    begin = {0: -TS}
    for p in range(3 * TS):
        if not low <= p - TS < high:
            down[0][p] = 0
    for level in (1, 2, 3):
        extent = 3 * TS >> level
        begin[level] = -(TS >> level)
        matrix = np.zeros((extent, 3 * TS))
        for i in range(extent):
            p = begin[level] + i
            if not (low >> level) <= p < (high >> level):
                continue
            for a, tap in enumerate(TAPS):
                source = 2 * p + a - 2 - begin[level - 1]
                if 0 <= source < down[level - 1].shape[0]:
                    matrix[i] += tap * down[level - 1][source]
        down[level] = matrix
    where = {entry: i for i, entry in enumerate(order)}
    d = np.zeros((TS, 3 * TS))
    for (level, p), i in where.items():
        d[i] = down[level][p - begin[level]]

    def grown(p):
        half = p // 2
        if p % 2 == 0:
            return ((half - 1, 0.125), (half, 0.75), (half + 1, 0.125))
        return ((half, 0.5), (half + 1, 0.5))

    up = np.zeros((TS, TS))
    for (level, p), i in where.items():
        if level < 3 and (low >> level) <= p < (high >> level):
            for q, weight in grown(p):
                up[i, where[(level + 1, q)]] += weight
    f = np.zeros((TS, TS))
    for p in range(TS):
        for q, weight in grown(p):
            f[p, where[(1, q)]] += weight
    q = f @ (np.eye(TS) + up + up @ up)
    return d, up, f, q


def bf16(x):
    return x.astype(ml_dtypes.bfloat16)


def tables():
    order = stack_order()
    levels = np.array([level for level, _ in order] + [0] * (TS - len(order)))
    same = ((levels[:, None] == levels[None, :]) & (levels[:, None] > 0)).astype(np.float32)
    dc, pc, qc, dr, pfr, qr = [], [], [], [], [], []
    for variant in range(4):
        d, up, f, q = operators(variant % 2 == 1, variant >= 2)
        mid = operators(False, False)[0]
        to_left = mid[8:16, 2 * TS :]
        to_right = mid[0:8, :TS]
        edges = np.concatenate([to_left, to_right])
        own = np.concatenate([d[:, TS : 2 * TS], edges])
        top = bf16(own).astype(np.float64)
        low = own - top
        three = np.concatenate([top, top, low], axis=1)
        assert np.all(bf16(low).astype(np.float64) == low)
        assert np.all(bf16(up).astype(np.float64) == up)
        q_top = bf16(q).astype(np.float64)
        q_three = np.concatenate([q_top, q_top, q - q_top], axis=1)
        dc.append(three)
        dr.append(three[:TS].T)
        pc.append(np.concatenate([up, up], axis=1))
        qc.append(q_three)
        pf = np.concatenate([up.T, f.T], axis=1)
        pfr.append(np.concatenate([pf, pf], axis=0))
        qr.append(q_three.T)
    de = dc[0][TS:]
    fc = np.concatenate([f, f], axis=1)
    return [bf16(np.stack(x)) for x in (dc, pc, qc, dr, pfr, qr)] + [bf16(de), bf16(fc), same]


def split(x, axis, three=False):
    top = x.astype(BF)
    low = (x - top.astype(F32)).astype(BF)
    return jnp.concatenate([top, low, top] if three else [top, low], axis=axis)


def dot(a, b):
    return jnp.dot(a, b, preferred_element_type=F32)


def regroup(x):
    row = lax.broadcasted_iota(jnp.int32, x.shape, 1)
    col = lax.broadcasted_iota(jnp.int32, x.shape, 2) // BS
    for d in (4, 2, 1):
        row_bit, col_bit = (row // d) % 2, (col // d) % 2
        ahead = pltpu.roll(pltpu.roll(x, 8 - d, 1), BS * d, 2)
        if d == 4:
            x = jnp.where(row_bit == col_bit, x, ahead)
        else:
            behind = pltpu.roll(pltpu.roll(x, d, 1), TS - BS * d, 2)
            x = jnp.where(row_bit == col_bit, x, jnp.where(row_bit == 0, ahead, behind))
    return x


def kernel(
    n_tx, n_ty, own, groups, spread, seats, strip,
    destination, offset, counts, scenes_h, cloud_h, *refs,
):
    consts_h, refs = refs[:9], refs[9:]
    out, refs = refs[0], refs[1:]
    consts, refs = refs[:9], refs[9:]
    dc, pc, qc, dr, pfr, qr, de, fc, same = consts
    (scenes, cloud, sent, landed, code_out, code_in, field, tiles, stack, deep, cols_out, cols_in, rows_out, rows_in,
     ratio, final, staged, strip_out, strip_in,
     const_sem, in_sem, block_send, block_recv, code_send, code_recv, halo_send, halo_recv, strip_send, strip_recv) = refs
    me, col = lax.axis_index("tx"), lax.axis_index("ty")
    chans = own + 1
    pixels = BS * BS
    variant_c = jnp.where(col == 0, 1, 0) + jnp.where(col == n_ty - 1, 2, 0)
    variant_r = jnp.where(me == 0, 1, 0) + jnp.where(me == n_tx - 1, 2, 0)
    fetch = [
        pltpu.make_async_copy(scenes_h.at[0], scenes, in_sem.at[0]),
        pltpu.make_async_copy(cloud_h.at[0], cloud, in_sem.at[1]),
    ]
    for f in fetch:
        f.start()

    barrier = pltpu.get_barrier_semaphore()
    for d in range(1, n_tx):
        pl.semaphore_signal(barrier, inc=1, device_id={"tx": lax.rem(me + d, n_tx)}, device_id_type=MESH)

    @pl.when(col > 0)
    def _():
        pl.semaphore_signal(barrier, inc=1, device_id={"ty": col - 1}, device_id_type=MESH)

    @pl.when(col < n_ty - 1)
    def _():
        pl.semaphore_signal(barrier, inc=1, device_id={"ty": col + 1}, device_id_type=MESH)

    variants = [variant_c] * 3 + [variant_r] * 3 + [None] * 3
    loads = [
        pltpu.make_async_copy(src if v is None else src.at[v], dst, const_sem.at[i])
        for i, (src, dst, v) in enumerate(zip(consts_h, consts, variants))
    ]
    for load in loads:
        load.start()

    dest = jnp.broadcast_to(destination[...], (S_DEV, S_DEV))
    lane = lax.broadcasted_iota(jnp.int32, (S_DEV, S_DEV), 1)
    sub = lax.broadcasted_iota(jnp.int32, (S_DEV, S_DEV), 0)
    live = jnp.broadcast_to(counts[...], (S_DEV, S_DEV))
    earlier = (dest == dest.T) & (sub < lane)
    rank = jnp.sum(jnp.where(earlier, 1.0, 0.0), axis=0, keepdims=True)
    target = jnp.where(lane[:1] < live[:1], dest[:1].astype(F32) * seats + rank, -1.0)
    seat_id = lax.broadcasted_iota(jnp.int32, (n_tx * seats, 1), 0).astype(F32)
    chooser = jnp.where(seat_id == target, 1.0, 0.0).astype(BF)

    lanes = lax.broadcasted_iota(jnp.int32, (S_DEV, TS), 1)
    rank_t = jnp.broadcast_to(rank, (S_DEV, S_DEV)).T[:, :1]
    seat = jnp.where(lanes.astype(F32) == rank_t, 1.0, 0.0).astype(BF)
    tall = lax.broadcasted_iota(jnp.int32, (max(16, n_tx), S_DEV), 0)
    across = lax.broadcasted_iota(jnp.int32, tall.shape, 1)
    marks = jnp.where((tall == destination[...]) & (across < counts[...]), (offset[...] + 1).astype(F32), 0.0)
    codes = dot(marks.astype(BF), seat)
    for t in range(n_tx):
        code_out[t] = jnp.broadcast_to(codes[t : t + 1], (8, TS))
    code_in[me] = code_out[me]

    def pack(first, last):
        for c in range(first, last):
            got = dot(chooser, cloud[...] if c == 0 else scenes[c - 1]).astype(BF)
            sent[:, c] = got.reshape(n_tx, seats, pixels)

    for f in reversed(fetch):
        f.wait()
    each = own // groups
    spans = [(0 if g == 0 else 1 + g * each, 1 + (g + 1) * each) for g in range(groups)]
    pack(*spans[0])
    pl.semaphore_wait(barrier, n_tx - 1 + jnp.where(col > 0, 1, 0) + jnp.where(col < n_ty - 1, 1, 0))

    def exchange(src, dst, send, recv, other, g=None, span=None, slot=None):
        slot = me if slot is None else slot
        if span is not None:
            src, dst = src.at[other, span[0] : span[1]], dst.at[slot, span[0] : span[1]]
            send, recv = send.at[g, other], recv.at[g, slot]
        elif g is not None:
            src, dst, send, recv = src.at[g, other], dst.at[g, slot], send.at[g, other], recv.at[g, slot]
        else:
            src, dst, send, recv = src.at[other], dst.at[slot], send.at[other], recv.at[slot]
        return pltpu.make_async_remote_copy(
            src_ref=src, dst_ref=dst, send_sem=send, recv_sem=recv, device_id={"tx": other}, device_id_type=MESH
        )

    peers = [lax.rem(me + d, n_tx) for d in range(1, n_tx)]
    code_refs = (code_out, code_in, code_send, code_recv)
    block_refs = (sent, landed, block_send, block_recv)
    strip_refs = (strip_out, strip_in, strip_send, strip_recv)
    for peer in peers:
        exchange(*code_refs, peer).start()
    for g, span in enumerate(spans):
        if g:
            pack(*span)
        for peer in peers:
            exchange(*block_refs, peer, g, span).start()
        landed[me, span[0] : span[1]] = sent[me, span[0] : span[1]]

    def halo(axis, src, dst, side, g, place_at, other, sending):
        span = slice(*spans[g])
        return pltpu.make_async_remote_copy(
            src_ref=src.at[side, span], dst_ref=dst.at[1 - side, span], send_sem=halo_send.at[g, place_at + side],
            recv_sem=halo_recv.at[g, place_at + 1 - side], device_id={axis: other}, device_id_type=MESH,
        )

    def swap(axis, at, n, src, dst, g, place_at):
        span = slice(*spans[g])

        @pl.when(at > 0)
        def _():
            halo(axis, src, dst, 0, g, place_at, at - 1, True).start()

        @pl.when(at < n - 1)
        def _():
            halo(axis, src, dst, 1, g, place_at, at + 1, True).start()

        @pl.when(at == 0)
        def _():
            dst[0, span] = jnp.zeros_like(dst[0, span])

        @pl.when(at == n - 1)
        def _():
            dst[1, span] = jnp.zeros_like(dst[1, span])

    def swapped(axis, at, n, src, dst, g, place_at):
        @pl.when(at > 0)
        def _():
            halo(axis, src, dst, 0, g, place_at, at - 1, True).wait_send()
            halo(axis, src, dst, 1, g, place_at, at - 1, False).wait_recv()

        @pl.when(at < n - 1)
        def _():
            halo(axis, src, dst, 1, g, place_at, at + 1, True).wait_send()
            halo(axis, src, dst, 0, g, place_at, at + 1, False).wait_recv()

    cols = ("ty", col, n_ty, cols_out, cols_in)
    line = ("tx", me, n_tx, rows_out, rows_in)
    landing = []

    def stage_a(g):
        first, last = spans[g]
        if g == 0:
            for peer in peers:
                exchange(*code_refs, peer, slot=peer).wait_recv()
            slot_id = lax.broadcasted_iota(jnp.int32, (SLOTS, 1), 0).astype(F32) + 1.0
            found = [jnp.where(slot_id == code_in[s][:1, :seats], 1.0, 0.0) for s in range(n_tx)]
            landing.append(jnp.concatenate(found * 2, axis=1).astype(BF))
        for peer in peers:
            exchange(*block_refs, peer, g, spans[g], slot=peer).wait_recv()
        cover = jnp.concatenate([landed[s, 0] for s in range(n_tx)], axis=0)
        wide = cover.astype(F32)
        for c in range(first, last):
            if c == 0:
                total = dot(landing[0][:, : n_tx * seats], cover)
            else:
                values = jnp.concatenate([landed[s, c] for s in range(n_tx)], axis=0).astype(F32)
                total = dot(landing[0], split(values * wide, 0))
            for half in range(2):
                part = total[:, half * TS : half * TS + TS].reshape(TS // BS, 8, TS)
                field[c, :, half] = regroup(part)
        for c in range(first, last):
            tile = field[c].reshape(TS, TS).T
            tiles[c] = tile
            if c == 0:
                for i in (0, 3, 6, 1, 2, 4, 5, 7, 8):
                    loads[i].wait()
            got = dot(dc[...], split(tile, 0, three=True))
            stack[c] = got[:TS]
            cols_out[0, c] = got[TS : TS + 8]
            cols_out[1, c] = got[TS + 8 : TS + 16]
        swap(*cols, g, 0)

    def stage_b(g):
        first, last = spans[g]
        swapped(*cols, g, 0)
        parts = []
        for c in range(first, last):
            whole = stack[c]
            parts += [whole[:8] + cols_in[0, c], whole[8:16] + cols_in[1, c], whole[16:]]
        flat = split(jnp.concatenate(parts, axis=0), 1, three=True)
        edges = lax.dot_general(de[...], flat, (((1,), (1,)), ((), ())), preferred_element_type=F32)
        for c in range(first, last):
            at = slice((c - first) * TS, (c - first + 1) * TS)
            rows_out[0, c] = edges[:8, at]
            rows_out[1, c] = edges[8:, at]
        swap(*line, g, 2)
        got = dot(flat, dr[...])
        for c in range(first, last):
            deep[c] = got[(c - first) * TS : (c - first + 1) * TS]

    def stage_c(g):
        first, last = spans[g]
        swapped(*line, g, 2)
        for c in range(first, last):
            rim = jnp.concatenate([rows_in[0, c], rows_in[1, c], jnp.zeros((TS - 16, TS), F32)], axis=0)
            deep[c] = deep[c] + rim.T
        if g == 0:
            ratio[0] = same[...] / (BACKGROUND + deep[0])
            ratio[1] = 1.0 / (BACKGROUND + tiles[0])
        mine = range(max(first, 1), last)
        whole = jnp.concatenate([deep[c] for c in mine], axis=0)
        detail = split(dot(split(whole, 1), pfr[...]), 1)
        bands = []
        finer = []
        for i, c in enumerate(mine):
            at = slice(i * TS, i * TS + TS)
            both = jnp.concatenate([detail[at, : 2 * TS], detail[at, 2 * TS :]], axis=0)
            bands.append((deep[c] - dot(pc[...], both[:, :TS])) * ratio[0])
            finer.append(dot(fc[...], both[:, TS:]))
        lifted = dot(split(jnp.concatenate(bands, axis=0), 1, three=True), qr[...])
        for i, c in enumerate(mine):
            at = slice(i * TS, i * TS + TS)
            final[i] = (tiles[c] - finer[i]) * ratio[1] + dot(qc[...], split(lifted[at], 0, three=True))
        for peer in peers:
            strip_out[g, peer] = strip_of(peer)
            exchange(*strip_refs, peer, g).start()
        strip_in[g, me] = strip_of(me)

    staged[...] = jnp.zeros_like(staged)

    def strip_of(t):
        for i in range(each):
            staged[i * strip : (i + 1) * strip, :] = final[i, pl.ds(t * strip, strip), :]
        return staged[...].astype(BF)

    for step in range(groups + 1):
        if step < groups:
            stage_a(step)
        if step > 0:
            stage_c(step - 1)
        if step < groups:
            stage_b(step)
    for g in range(groups):
        for peer in peers:
            exchange(*strip_refs, peer, g, slot=peer).wait_recv()
        for s in range(n_tx):
            got = strip_in[g, s].astype(F32)
            for i in range(each):
                out[g * each + i, 0, :, s * TS : (s + 1) * TS] = got[i * strip : (i + 1) * strip].astype(BF)
    for peer in peers:
        exchange(*code_refs, peer).wait_send()
        for g in range(groups):
            exchange(*block_refs, peer, g, spans[g]).wait_send()
            exchange(*strip_refs, peer, g).wait_send()


def solution(mesh):
    n_tx, n_ty = mesh.shape["tx"], mesh.shape["ty"]
    consts = tables()

    def local(scenes, cloud, destination, offset, counts):
        own = scenes.shape[2]
        chans = own + 1
        groups = 3 if own % 3 == 0 else 1
        each = own // groups
        spread = max(2, 2 * S_DEV // n_tx)
        seats = -(-spread // 16) * 16
        strip = TS // n_tx
        strip_rows = -(-each * strip // 16) * 16
        pixels = BS * BS
        vmem = pl.BlockSpec(memory_space=pltpu.VMEM)
        hbm = pl.BlockSpec(memory_space=pltpu.HBM)
        dma = pltpu.SemaphoreType.DMA
        return pl.pallas_call(
            functools.partial(kernel, n_tx, n_ty, own, groups, spread, seats, strip),
            out_shape=jax.ShapeDtypeStruct((own, 1, strip, TS * n_tx), BF),
            in_specs=[vmem] * 3 + [hbm] * 11,
            out_specs=vmem,
            scratch_shapes=[pltpu.VMEM(x.shape[1:], BF) for x in consts[:6]]
            + [pltpu.VMEM(x.shape, BF) for x in consts[6:8]]
            + [
                pltpu.VMEM((TS, TS), F32),
                pltpu.VMEM((own, S_DEV, pixels), BF),
                pltpu.VMEM((S_DEV, pixels), BF),
                pltpu.VMEM((n_tx, chans, seats, pixels), BF),
                pltpu.VMEM((n_tx, chans, seats, pixels), BF),
                pltpu.VMEM((n_tx, 8, TS), F32),
                pltpu.VMEM((n_tx, 8, TS), F32),
                pltpu.VMEM((chans, TS // BS, 2, 8, TS), F32),
                pltpu.VMEM((chans, TS, TS), F32),
                pltpu.VMEM((chans, TS, TS), F32),
                pltpu.VMEM((chans, TS, TS), F32),
                pltpu.VMEM((2, chans, 8, TS), F32),
                pltpu.VMEM((2, chans, 8, TS), F32),
                pltpu.VMEM((2, chans, 8, TS), F32),
                pltpu.VMEM((2, chans, 8, TS), F32),
                pltpu.VMEM((2, TS, TS), F32),
                pltpu.VMEM((each, TS, TS), F32),
                pltpu.VMEM((strip_rows, TS), F32),
                pltpu.VMEM((groups, n_tx, strip_rows, TS), BF),
                pltpu.VMEM((groups, n_tx, strip_rows, TS), BF),
                dma((9,)), dma((2,)),
                dma((groups, n_tx)), dma((groups, n_tx)), dma((n_tx,)), dma((n_tx,)),
                dma((groups, 4)), dma((groups, 4)), dma((groups, n_tx)), dma((groups, n_tx)),
            ],
            compiler_params=pltpu.CompilerParams(
                collective_id=0, has_side_effects=True, vmem_limit_bytes=62 * 1024 * 1024
            ),
        )(destination, offset, counts, jnp.swapaxes(scenes, 1, 2), cloud, *(jnp.asarray(x) for x in consts))

    placed = (
        P(("region", "ty"), "tx", "band", None),
        P(("region", "ty"), "tx", None),
        P(("region", "ty"), "tx"),
        P(("region", "ty"), "tx"),
        P(("region", "ty"), "tx"),
    )
    return jax.shard_map(
        local, mesh=mesh, in_specs=placed, out_specs=P("band", ("region", "ty"), "tx", None), check_vma=False
    )
```

time: 41.6 us -> 37.6 us (0.904)
  local copies, waits for them, and re-layouts: 9.17 us -> 1.62 us
  Pallas kernels: 31.2 us -> 35.2 us
    unnamed x26 -> x1, local copies, waits for them, and re-layouts: 9.17 us -> 1.62 us
    pallas_call x1, Pallas kernels: 31.2 us -> 35.2 us  [local(): pl.pallas_call(functools.partial(kernel, n_tx, n_ty, own, groups, spread,...]
where the time goes in v2:
time: 37.6 us; the launch traced here: 37.5 us
  Pallas kernels  35.2 us (94%)
  local copies, waits for them, and re-layouts  1.62 us (4%)
  between operations  0.66 us (2%)
    pallas_call x1, Pallas kernels, local(): pl.pallas_call(functools.partial(kernel, n_tx, n_ty, own, groups, spread,...  35.2 us
    unnamed x1, local copies, waits for them, and re-layouts  1.62 us

profile of v2, /device:TPU:0, one launch (start us, length us, event | category | flops | bytes accessed | tf_op | source)
XLA Modules:
  0.0 37.5 jit_solution(10770049083548889760)
XLA Ops:
  0.7 35.2 %shard_map.136 = bf16[6,1,32,512]{3,2,1,0:T(8,128)(2,1)} custom-call(s32[1,64]{1,0:T(1,128)} %destination.1, s32[1,64]{1,0:T(1,128)} %offset.1, s32[1,1]{1,0:T(1,128)S(6)} %copy.16.counts, bf16[1,6,64,256]{3,2,1,0:T(8,128)(2,1)} %bitcast.1, bf16[1,64,256]{2,1,0:T(8,128)(2,1)} %cloud_h.1, bf16[4,144,384]{2,1,0:T(8,128)(2,1)} %constant.18.clone.refs_0_, ...), custom_call_target="tpu_custom_call" | custom-call | tf_op jit(solution)/shard_map/pallas_call | solution.py:411
  35.8 1.6 %copy.17 = bf16[6,1,32,512]{3,2,1,0:T(8,128)(2,1)} copy(bf16[6,1,32,512]{3,2,1,0:T(8,128)(2,1)} %shard_map.136) | data formatting | bytes 393216

commit v3 on v2

--- a/solution.py
+++ b/solution.py
@@ -239,8 +239,9 @@
     for g, span in enumerate(spans):
         if g:
             pack(*span)
-        for peer in peers:
-            exchange(*block_refs, peer, g, span).start()
+        else:
+            for peer in peers:
+                exchange(*block_refs, peer, g, span).start()
         landed[me, span[0] : span[1]] = sent[me, span[0] : span[1]]
 
     def halo(axis, src, dst, side, g, place_at, other, sending):
@@ -292,6 +293,10 @@
             slot_id = lax.broadcasted_iota(jnp.int32, (SLOTS, 1), 0).astype(F32) + 1.0
             found = [jnp.where(slot_id == code_in[s][:1, :seats], 1.0, 0.0) for s in range(n_tx)]
             landing.append(jnp.concatenate(found * 2, axis=1).astype(BF))
+        for peer in peers:
+            exchange(*block_refs, peer, g, spans[g]).wait_send()
+            if g + 1 < groups:
+                exchange(*block_refs, peer, g + 1, spans[g + 1]).start()
         for peer in peers:
             exchange(*block_refs, peer, g, spans[g], slot=peer).wait_recv()
         cover = jnp.concatenate([landed[s, 0] for s in range(n_tx)], axis=0)
@@ -370,13 +375,13 @@
             staged[i * strip : (i + 1) * strip, :] = final[i, pl.ds(t * strip, strip), :]
         return staged[...].astype(BF)
 
-    for step in range(groups + 1):
+    for step in range(groups + 2):
         if step < groups:
             stage_a(step)
-        if step > 0:
-            stage_c(step - 1)
-        if step < groups:
-            stage_b(step)
+        if 0 < step <= groups:
+            stage_b(step - 1)
+        if step > 1:
+            stage_c(step - 2)
     for g in range(groups):
         for peer in peers:
             exchange(*strip_refs, peer, g, slot=peer).wait_recv()
@@ -387,7 +392,6 @@
     for peer in peers:
         exchange(*code_refs, peer).wait_send()
         for g in range(groups):
-            exchange(*block_refs, peer, g, spans[g]).wait_send()
             exchange(*strip_refs, peer, g).wait_send()
 
 
@@ -398,7 +402,7 @@
     def local(scenes, cloud, destination, offset, counts):
         own = scenes.shape[2]
         chans = own + 1
-        groups = 3 if own % 3 == 0 else 1
+        groups = 2 if own % 2 == 0 else 1
         each = own // groups
         spread = max(2, 2 * S_DEV // n_tx)
         seats = -(-spread // 16) * 16

time: 37.6 us -> 32.6 us (0.87)
  Pallas kernels: 35.2 us -> 30.1 us
    pallas_call x1, Pallas kernels: 35.2 us -> 30.1 us  [local(): pl.pallas_call(functools.partial(kernel, n_tx, n_ty, own, groups, spread,...]
where the time goes in v3:
time: 32.6 us; the launch traced here: 32.4 us
  Pallas kernels  30.1 us (92%)
  local copies, waits for them, and re-layouts  1.62 us (5%)
  between operations  0.66 us (2%)
    pallas_call x1, Pallas kernels, local(): pl.pallas_call(functools.partial(kernel, n_tx, n_ty, own, groups, spread,...  30.1 us
    unnamed x1, local copies, waits for them, and re-layouts  1.62 us

profile of v3, /device:TPU:0, one launch (start us, length us, event | category | flops | bytes accessed | tf_op | source)
XLA Modules:
  0.0 32.4 jit_solution(14949644541611070051)
XLA Ops:
  0.7 30.1 %shard_map.136 = bf16[6,1,32,512]{3,2,1,0:T(8,128)(2,1)} custom-call(s32[1,64]{1,0:T(1,128)} %destination.1, s32[1,64]{1,0:T(1,128)} %offset.1, s32[1,1]{1,0:T(1,128)S(6)} %copy.16.counts, bf16[1,6,64,256]{3,2,1,0:T(8,128)(2,1)} %bitcast.1, bf16[1,64,256]{2,1,0:T(8,128)(2,1)} %cloud_h.1, bf16[4,144,384]{2,1,0:T(8,128)(2,1)} %constant.18.clone.refs_0_, ...), custom_call_target="tpu_custom_call" | custom-call | tf_op jit(solution)/shard_map/pallas_call | solution.py:415
  30.8 1.6 %copy.17 = bf16[6,1,32,512]{3,2,1,0:T(8,128)(2,1)} copy(bf16[6,1,32,512]{3,2,1,0:T(8,128)(2,1)} %shard_map.136) | data formatting | bytes 393216

commit v4 on v3

--- a/solution.py
+++ b/solution.py
@@ -239,9 +239,8 @@
     for g, span in enumerate(spans):
         if g:
             pack(*span)
-        else:
-            for peer in peers:
-                exchange(*block_refs, peer, g, span).start()
+        for peer in peers:
+            exchange(*block_refs, peer, g, span).start()
         landed[me, span[0] : span[1]] = sent[me, span[0] : span[1]]
 
     def halo(axis, src, dst, side, g, place_at, other, sending):
@@ -295,8 +294,6 @@
             landing.append(jnp.concatenate(found * 2, axis=1).astype(BF))
         for peer in peers:
             exchange(*block_refs, peer, g, spans[g]).wait_send()
-            if g + 1 < groups:
-                exchange(*block_refs, peer, g + 1, spans[g + 1]).start()
         for peer in peers:
             exchange(*block_refs, peer, g, spans[g], slot=peer).wait_recv()
         cover = jnp.concatenate([landed[s, 0] for s in range(n_tx)], axis=0)

time: 32.6 us -> 32.4 us (level)
  no operation moved by 1% of the time
where the time goes in v4:
time: 32.4 us; the launch traced here: 32.2 us
  Pallas kernels  30 us (93%)
  local copies, waits for them, and re-layouts  1.62 us (5%)
  between operations  0.66 us (2%)
    pallas_call x1, Pallas kernels, local(): pl.pallas_call(functools.partial(kernel, n_tx, n_ty, own, groups, spread,...  30 us
    unnamed x1, local copies, waits for them, and re-layouts  1.62 us

profile of v4, /device:TPU:0, one launch (start us, length us, event | category | flops | bytes accessed | tf_op | source)
XLA Modules:
  0.0 32.2 jit_solution(16993768322692734808)
XLA Ops:
  0.7 30.0 %shard_map.136 = bf16[6,1,32,512]{3,2,1,0:T(8,128)(2,1)} custom-call(s32[1,64]{1,0:T(1,128)} %destination.1, s32[1,64]{1,0:T(1,128)} %offset.1, s32[1,1]{1,0:T(1,128)S(6)} %copy.16.counts, bf16[1,6,64,256]{3,2,1,0:T(8,128)(2,1)} %bitcast.1, bf16[1,64,256]{2,1,0:T(8,128)(2,1)} %cloud_h.1, bf16[4,144,384]{2,1,0:T(8,128)(2,1)} %constant.18.clone.refs_0_, ...), custom_call_target="tpu_custom_call" | custom-call | tf_op jit(solution)/shard_map/pallas_call | solution.py:412
  30.6 1.6 %copy.17 = bf16[6,1,32,512]{3,2,1,0:T(8,128)(2,1)} copy(bf16[6,1,32,512]{3,2,1,0:T(8,128)(2,1)} %shard_map.136) | data formatting | bytes 393216
